TPU v7x, 512 devices: a whole 4x4x16 slice. The times are simulated.
512 devices in a mesh: gx: 16 (over y_lo, x, core), gy: 32 (over z, y_hi).
Axes of the slice: x: 4, y: 4 (y_hi: 2, y_lo: 2; y = y_hi * 2 + y_lo), z: 16, core: 2. Of those that a mesh axis runs over, the one named last changes fastest.
Arguments:
- forcing: float32 [64, 64, 2, 4096], P('gx', 'gy'), may hold values from -6 to 6
- initial: float32 [64, 64, 2, 4096], P('gx', 'gy'), may hold values from -6 to 6
- blocks: float32 [64, 64, 2, 4096], P('gx', 'gy'), as said below
- face_blocks: float32 [6, 64, 64], replicated, may hold values from -0.75 to 0.75
- strength: float32 [6, 64, 64, 2], P(None, 'gx', 'gy'), may hold values from 0.2 to 2
- strong: int32 [6, 64, 64, 2], P(None, 'gx', 'gy'), may hold values 0 or 1
- colour: int32 [64, 64, 2], P('gx', 'gy'), may hold values from 0 to 1, as said below
- neighbours: int32 [6, 64, 64, 2], P(None, 'gx', 'gy'), may hold values from 2 to 48, as said below
Outputs:
- smoothed: float32 [64, 64, 2, 4096], P('gx', 'gy')
Inputs may be any that keep to these rules, and one draw needn't show every extreme that they name: Elements of a column along z are stored in an order drawn per column. colour is (global x index + global y index + physical position along z + one flip common to all elements) mod 2, so elements that share a face differ in colour and every column holds one element of each colour. `neighbours`: Slots of the four corner columns are never named. `blocks`: each block is symmetric, and each diagonal entry exceeds the sum of the magnitudes of the other entries of its row by 0.5 or more.
All inputs are finite; a program needn't handle non-finite values. No bound on the sum of `strong` on one device may be relied on, other than what follows from the above.
Results may differ from a plain program's by a relative error of at most 0.00011.
Values sent between devices are 32-bit elements; how exact they have to be, the bound alone decides.
A program may use at most 64 MiB of HBM per device.

v0:
```python
import jax
import jax.numpy as jnp
from jax import lax
from jax.experimental import pallas as pl
from jax.experimental.pallas import tpu as pltpu
from jax.sharding import PartitionSpec as P

MESH = pl.DeviceIdType.MESH
N = 64
STEPS = 8
F32 = jnp.float32
BF16 = jnp.bfloat16


def left_lanes(shape):
    return lax.broadcasted_iota(jnp.int32, shape, len(shape) - 1) < N


def swap(tile):
    return pltpu.roll(tile, N, tile.ndim - 1)


def parts(value):
    high = value.astype(BF16)
    return high, (value - high.astype(F32)).astype(BF16)


def unpack_pair(source, rows, store, bank, b, h, paint):
    halves = []
    for low in range(2):
        a = 2 * h + low
        first = rows[pl.ds(a * 2 + b, 1), pl.ds(6 * N, 128)] * jnp.ones((32, 1), F32)
        zero = source[a, b, pl.ds(0, 32, stride=2), :]
        one = source[a, b, pl.ds(1, 32, stride=2), :]
        wanted = first == paint
        halves.append(jnp.where(wanted, zero, one))
    left = left_lanes((32, 128))
    even = jnp.where(left, halves[0], swap(halves[1]))
    odd = jnp.where(left, swap(halves[0]), halves[1])
    store[bank, b, h, pl.ds(0, 32, stride=2), :] = even
    store[bank, b, h, pl.ds(1, 32, stride=2), :] = odd


def invert(grid):
    pairs = grid.shape[0]
    lane = lax.broadcasted_iota(jnp.int32, (8, 128), 1)
    row = lax.broadcasted_iota(jnp.int32, (8, 128), 0)
    within = lax.rem(lane, N)
    start = lane - within

    def pick(tile, index):
        return jnp.take_along_axis(tile, index, axis=1)

    def block(k, carry):
        panels = [grid[e, pl.ds(pl.multiple_of(8 * k, 8), 8), :] for e in range(pairs)]
        for j in range(8):
            column = 8 * k + j
            index = start + column
            here = within == column
            for e in range(pairs):
                panel = panels[e]
                pivot_row = jnp.broadcast_to(panel[j : j + 1, :], (8, 128))
                factor = pick(panel, index)
                scale = 1.0 / pick(pivot_row, index)
                scaled = jnp.where(here, 1.0, pivot_row) * scale
                rest = jnp.where(here, 0.0, panel) - factor * scaled
                panels[e] = jnp.where(row == j, scaled, rest)
        inside = (within >= 8 * k) & (within < 8 * k + 8)
        for e in range(pairs):
            panel = panels[e]

            def group(g, carry, e=e, panel=panel):
                at = pl.ds(pl.multiple_of(8 * g, 8), 8)
                old = grid[e, at, :]
                total = jnp.where(inside, 0.0, old)
                for j in range(8):
                    total = total - pick(old, start + 8 * k + j) * jnp.broadcast_to(
                        panel[j : j + 1, :], (8, 128)
                    )
                grid[e, at, :] = total
                return carry

            lax.fori_loop(0, 8, group, 0, unroll=True)
            grid[e, pl.ds(pl.multiple_of(8 * k, 8), 8), :] = panel
        return carry

    lax.fori_loop(0, 8, block, 0)


def kernel(
    forcing, initial, blocks, faces, rows, out,
    state, cross, halo, grid, couple, source_term, spread, send_sem, recv_sem,
):
    gx, gy = lax.axis_index("gx"), lax.axis_index("gy")
    nx, ny = lax.axis_size("gx"), lax.axis_size("gy")
    x_low, x_high = (lax.rem(gx + nx - 1, nx), gy), (lax.rem(gx + 1, nx), gy)
    y_low, y_high = (gx, lax.rem(gy + ny - 1, ny)), (gx, lax.rem(gy + 1, ny))
    barrier = pltpu.get_barrier_semaphore()
    for device in (x_low, x_high, y_low, y_high):
        pl.semaphore_signal(barrier, inc=1, device_id=device, device_id_type=MESH)
    left = left_lanes((N, 128))

    def copies(t):
        def copy(slot, source, device):
            return pltpu.make_async_remote_copy(
                src_ref=source,
                dst_ref=halo.at[t, slot],
                send_sem=send_sem.at[t, slot],
                recv_sem=recv_sem.at[t, slot],
                device_id=device,
                device_id_type=MESH,
            )

        return [
            copy(0, state.at[t, 1, 0], y_high),
            copy(1, state.at[t, 1, 1], y_high),
            copy(2, state.at[t, 0, 0], y_low),
            copy(3, state.at[t, 0, 1], y_low),
            copy(4, cross.at[t, 0], x_high),
            copy(5, cross.at[t, 1], x_low),
        ]

    def prepare(t):
        cross[t, 0] = jnp.where(left, swap(state[t, 0, 1]), state[t, 1, 1])
        cross[t, 1] = jnp.where(left, state[t, 0, 0], swap(state[t, 1, 0]))

    for b in range(2):
        for h in range(2):
            unpack_pair(initial, rows, state, 0, b, h, 0.0)
    prepare(0)
    pl.semaphore_wait(barrier, 4)
    for copy in copies(0):
        copy.start()

    for c in range(2):
        for b in range(2):
            for h in range(2):
                unpack_pair(blocks, rows, grid, c, b, h, 1.0 - c)
                unpack_pair(forcing, rows, source_term, c, b, h, 1.0 - c)
    invert(grid.reshape(8, N, 128))

    for i in range(3):
        both = jnp.concatenate([faces[2 * i], faces[2 * i + 1]], axis=1)
        high, low = parts(both)
        for half in range(2):
            at = pl.ds(half * N, N)
            spread[at, pl.ds(128 * i, 128)] = high
            spread[at, pl.ds(384 + 128 * i, 128)] = low

    def setup(i, carry):
        c, b, h = i // 4, lax.rem(i // 2, 2), lax.rem(i, 2)
        inverse = grid[c, b, h]
        stacked = jnp.concatenate(
            [jnp.where(left, inverse, 0.0), jnp.where(left, 0.0, inverse)], axis=0
        )
        high, low = parts(stacked)
        operand = jnp.concatenate([high, low], axis=0)
        folded = jnp.dot(operand, spread[...], preferred_element_type=F32)
        product = folded[:128, :384] + (folded[128:, :384] + folded[:128, 384:])
        target = source_term[c, b, h]
        t_high, t_low = parts(jnp.concatenate([target, target], axis=0))
        folded = jnp.dot(
            operand, jnp.concatenate([t_high, t_low], axis=1), preferred_element_type=F32
        )
        known = folded[:128, :128] + (folded[128:, :128] + folded[:128, 128:])
        source_term[c, b, h] = jnp.where(left, known[:N], known[N:])
        for low_x in range(2):
            e = c * 8 + (2 * h + low_x) * 2 + b
            scaled = product[N * low_x : N * low_x + N] * rows[pl.ds(e, 1), pl.ds(0, 384)]
            high, low = parts(scaled)
            couple[c, b, h, pl.ds(128 * low_x, N), :] = high
            couple[c, b, h, pl.ds(128 * low_x + N, N), :] = low
        return carry

    lax.fori_loop(0, 8, setup, 0)

    def step(t, c):
        for copy in copies(t):
            copy.wait_recv()
        x_before, x_after = halo[t, 4], halo[t, 5]
        for b in range(2):
            one, two = state[t, b, 0], state[t, b, 1]
            if b == 0:
                before, after = x_before, swap(x_after)
            else:
                before, after = swap(x_before), x_after
            slides = [
                jnp.where(left, before, swap(one)),
                swap(jnp.where(left, two, one)),
                jnp.where(left, swap(two), after),
            ]
            for h in range(2):
                y_before = halo[t, h] if b == 0 else state[t, 0, h]
                y_after = state[t, 1, h] if b == 0 else halo[t, 2 + h]
                own = state[t, b, h]
                near = jnp.concatenate(
                    [slides[h], slides[h + 1], y_before, y_after, own, own], axis=0
                )
                high, low = parts(near)
                total = jnp.dot(
                    couple[c, b, h],
                    jnp.concatenate([high, low], axis=1),
                    preferred_element_type=F32,
                )
                first = total[:N, :128] + (total[N:128, :128] + total[:N, 128:])
                second = total[128:192, :128] + (total[192:, :128] + total[128:192, 128:])
                state[t + 1, b, h] = source_term[c, b, h] - jnp.where(left, first, second)

    def sweep(t, carry):
        step(t, lax.rem(t, 2))
        prepare(t + 1)
        for copy in copies(t + 1):
            copy.start()
        return carry

    lax.fori_loop(0, STEPS - 1, sweep, 0)
    step(STEPS - 1, 1)

    small = left_lanes((32, 128))
    for b in range(2):
        for h in range(2):
            values = []
            for c in range(2):
                even = state[STEPS - 1 + c, b, h, pl.ds(0, 32, stride=2), :]
                odd = state[STEPS - 1 + c, b, h, pl.ds(1, 32, stride=2), :]
                values.append(
                    (jnp.where(small, even, swap(odd)), jnp.where(small, swap(even), odd))
                )
            for low_x in range(2):
                a = 2 * h + low_x
                first = rows[pl.ds(a * 2 + b, 1), pl.ds(6 * N, 128)] * jnp.ones((32, 1), F32)
                zero, one = values[0][low_x], values[1][low_x]
                out[a, b, pl.ds(0, 32, stride=2), :] = jnp.where(first == 1.0, zero, one)
                out[a, b, pl.ds(1, 32, stride=2), :] = jnp.where(first == 1.0, one, zero)

    def drain(t, carry):
        for copy in copies(t):
            copy.wait_send()
        return carry

    lax.fori_loop(0, STEPS, drain, 0)


def body(forcing, initial, blocks, face_blocks, strength, strong, colour, neighbours):
    sx, sy, sz, width = forcing.shape
    chunks = width // 128

    def packed(array):
        split = array.reshape(sx, sy, sz, chunks, 128).transpose(0, 1, 3, 2, 4)
        return split.reshape(sx, sy, chunks * sz, 128)

    weight = jnp.where(neighbours == 48, 0.0, strength * strong.astype(F32))
    zero_first = (colour[:, :, 0] == 0)[None]
    by_colour = jnp.stack(
        [
            jnp.where(zero_first, weight[..., 0], weight[..., 1]),
            jnp.where(zero_first, weight[..., 1], weight[..., 0]),
        ]
    )
    rows = jnp.repeat(by_colour.transpose(0, 2, 3, 1).reshape(16, 6), N, axis=1)
    first = jnp.broadcast_to(zero_first[0].astype(F32).reshape(1, 8, 1), (2, 8, 128))
    rows = jnp.concatenate([rows, first.reshape(16, 128)], axis=1)

    vmem = pl.BlockSpec(memory_space=pltpu.VMEM)
    result = pl.pallas_call(
        kernel,
        out_shape=jax.ShapeDtypeStruct((sx, sy, chunks * sz, 128), F32),
        in_specs=[vmem] * 5,
        out_specs=vmem,
        scratch_shapes=[
            pltpu.VMEM((STEPS + 1, 2, 2, N, 128), F32),
            pltpu.VMEM((STEPS, 2, N, 128), F32),
            pltpu.VMEM((STEPS, 6, N, 128), F32),
            pltpu.VMEM((2, 2, 2, N, 128), F32),
            pltpu.VMEM((2, 2, 2, 4 * N, 6 * N), BF16),
            pltpu.VMEM((2, 2, 2, N, 128), F32),
            pltpu.VMEM((2 * N, 12 * N), BF16),
            pltpu.SemaphoreType.DMA((STEPS, 6)),
            pltpu.SemaphoreType.DMA((STEPS, 6)),
        ],
        compiler_params=pltpu.CompilerParams(
            collective_id=0, has_side_effects=True, vmem_limit_bytes=40 * 2**20
        ),
    )(packed(forcing), packed(initial), packed(blocks), face_blocks, rows)
    result = result.reshape(sx, sy, chunks, sz, 128).transpose(0, 1, 3, 2, 4)
    return result.reshape(sx, sy, sz, width)


def solution(mesh):
    in_specs = (
        P("gx", "gy", None, None),
        P("gx", "gy", None, None),
        P("gx", "gy", None, None),
        P(),
        P(None, "gx", "gy", None),
        P(None, "gx", "gy", None),
        P("gx", "gy", None),
        P(None, "gx", "gy", None),
    )
    out_specs = P("gx", "gy", None, None)
    return jax.shard_map(body, mesh=mesh, in_specs=in_specs, out_specs=out_specs, check_vma=False)
```

profile of v0, /device:TPU:6, one launch (start us, length us, event | category | flops | bytes accessed | tf_op | source)
XLA Modules:
  0.0 82.2 jit_solution(5757027387676050786)
XLA Ops:
  0.0 0.0 copy-start
  0.0 0.7 slice.11
  0.7 0.1 copy.38
  0.8 0.1 reshape.94
  0.9 0.1 broadcast_in_dim.32
  1.0 0.1 broadcast_in_dim.33
  1.1 0.7 compare_select_fusion
  1.8 0.1 bitcast_select_fusion.1
  1.9 0.1 broadcast_in_dim.30
  2.0 0.1 reshape.91
  2.1 0.0 copy-done
  2.1 0.0 copy-start.1
  2.1 0.9 %copy-done.1 = f32[4,2,2,4096]{3,2,1,0:T(2,128)S(1)} copy-done((f32[4,2,2,4096]{3,2,1,0:T(2,128)S(1)}, f32[4,2,2,4096]{3,2,1,0:T(2,128)}, u32[]{:S(2)}) %copy-start.1) | copy-done | bytes 262168
  3.1 0.0 copy-start.2
  3.1 0.9 %copy-done.2 = f32[4,2,2,4096]{3,2,1,0:T(2,128)S(1)} copy-done((f32[4,2,2,4096]{3,2,1,0:T(2,128)S(1)}, f32[4,2,2,4096]{3,2,1,0:T(2,128)}, u32[]{:S(2)}) %copy-start.2) | copy-done | bytes 262168
  4.0 0.0 copy-start.3
  4.0 0.9 %copy-done.3 = f32[6,64,64]{2,1,0:T(8,128)S(1)} copy-done((f32[6,64,64]{2,1,0:T(8,128)S(1)}, f32[6,64,64]{2,1,0:T(8,128)}, u32[]{:S(2)}) %copy-start.3) | copy-done | bytes 98328
  4.9 76.6 %shard_map.82 = f32[4,2,64,128]{3,2,1,0:T(8,128)S(1)} custom-call(f32[4,2,64,128]{3,2,1,0:T(8,128)S(1)} %bitcast.35, f32[4,2,64,128]{3,2,1,0:T(8,128)S(1)} %bitcast.36, f32[4,2,64,128]{3,2,1,0:T(8,128)S(1)} %bitcast.37, f32[6,64,64]{2,1,0:T(8,128)S(1)} %copy-done.3, f32[16,512]{1,0:T(8,128)S(1)} %pad_maximum_fusion.rows), custom_call_target="tpu_custom_call" | custom-call | tf_op jit(solution)/shard_map/pallas_call | solution.py:265
  81.5 0.7 copy.47
  (6 shorter events, 0.0 us)
Async XLA Ops:
  0.0 2.1 %copy-start = (f32[4,2,2,4096]{3,2,1,0:T(2,128)S(1)}, f32[4,2,2,4096]{3,2,1,0:T(2,128)}, u32[]{:S(2)}) copy-start(f32[4,2,2,4096]{3,2,1,0:T(2,128)} %param.8) | copy-start | bytes 786436
  2.1 1.0 %copy-start.1 = (f32[4,2,2,4096]{3,2,1,0:T(2,128)S(1)}, f32[4,2,2,4096]{3,2,1,0:T(2,128)}, u32[]{:S(2)}) copy-start(f32[4,2,2,4096]{3,2,1,0:T(2,128)} %param.9) | copy-start | bytes 786436
  3.1 0.9 %copy-start.2 = (f32[4,2,2,4096]{3,2,1,0:T(2,128)S(1)}, f32[4,2,2,4096]{3,2,1,0:T(2,128)}, u32[]{:S(2)}) copy-start(f32[4,2,2,4096]{3,2,1,0:T(2,128)} %param.10) | copy-start | bytes 786436
  4.0 0.9 %copy-start.3 = (f32[6,64,64]{2,1,0:T(8,128)S(1)}, f32[6,64,64]{2,1,0:T(8,128)}, u32[]{:S(2)}) copy-start(f32[6,64,64]{2,1,0:T(8,128)} %faces.1) | copy-start | bytes 294916
where the time goes:
time: 82.5 us; the launch traced here: 82.2 us
  Pallas kernels  76.6 us (93%)
  local copies, waits for them, and re-layouts  4.78 us (6%)
  other arithmetic  0.84 us (1%)
    pallas_call x1, Pallas kernels, body(): pl.pallas_call(kernel, out_shape=jax.ShapeDtypeStruct((sx, sy, chunks * s...  76.6 us
    unnamed x9, local copies, waits for them, and re-layouts  3.54 us

commit v1 on v0

v1 whole, which is shorter than its diff:
```python
import jax
import jax.numpy as jnp
from jax import lax
from jax.experimental import pallas as pl
from jax.experimental.pallas import tpu as pltpu
from jax.sharding import PartitionSpec as P

MESH = pl.DeviceIdType.MESH
N = 64
STEPS = 8
GREET = 2
F32 = jnp.float32
BF16 = jnp.bfloat16


def left_lanes(shape):
    return lax.broadcasted_iota(jnp.int32, shape, len(shape) - 1) < N


def swap(tile):
    return pltpu.roll(tile, N, tile.ndim - 1)


def pick(tile, index):
    return jnp.take_along_axis(tile, index, axis=1)


def spread_row(tile, j):
    return jnp.broadcast_to(tile[j : j + 1, :], tile.shape)


def parts(value):
    high = value.astype(BF16)
    return high, (value - high.astype(F32)).astype(BF16)


def product(operand, value):
    high, low = parts(value)
    total = jnp.dot(
        operand, jnp.concatenate([high, low], axis=1), preferred_element_type=F32
    )
    first = total[:N, :128] + (total[N:128, :128] + total[:N, 128:])
    second = total[128:192, :128] + (total[192:, :128] + total[128:192, 128:])
    return jnp.where(left_lanes((N, 128)), first, second)


def unpack_pair(source, rows, target, b, h, paint):
    halves = []
    for low in range(2):
        a = 2 * h + low
        first = jnp.broadcast_to(rows[pl.ds(a * 2 + b, 1), pl.ds(384, 128)], (32, 128))
        zero = source[a, b, pl.ds(0, 32, stride=2), :]
        one = source[a, b, pl.ds(1, 32, stride=2), :]
        halves.append(jnp.where(first == paint, zero, one))
    left = left_lanes((32, 128))
    target[b, h, pl.ds(0, 32, stride=2), :] = jnp.where(left, halves[0], swap(halves[1]))
    target[b, h, pl.ds(1, 32, stride=2), :] = jnp.where(left, swap(halves[0]), halves[1])


def invert(grid, visit):
    places = [(b, h) for b in range(2) for h in range(2)]
    lane = lax.broadcasted_iota(jnp.int32, (8, 128), 1)
    row = lax.broadcasted_iota(jnp.int32, (8, 128), 0)
    within = lax.rem(lane, N)
    start = lane - within
    segment = within // 16

    def block(k, carry):
        visit(k)
        here = pl.ds(pl.multiple_of(8 * k, 8), 8)
        panels = [grid[b, h, here, :] for b, h in places]
        columns = []
        for j in range(8):
            index = start + 8 * k + j
            column = pick(panels[3], index)
            for e in range(3):
                column = jnp.where(segment == e, pick(panels[e], index), column)
            columns.append(column)
        for k2 in range(8):
            pivots = [spread_row(column, k2) for column in columns]
            scale = 1.0 / pivots[k2]
            factor = columns[k2]
            for j in range(8):
                scaled = scale if j == k2 else pivots[j] * scale
                rest = -(factor * scaled) if j == k2 else columns[j] - factor * scaled
                columns[j] = jnp.where(row == k2, scaled, rest)
        inside = (within >= 8 * k) & (within < 8 * k + 8)
        ones = within - 8 * k
        for e, (b, h) in enumerate(places):
            own = [pick(column, start + 16 * e) for column in columns]
            panel = jnp.zeros((8, 128), F32)
            for j in range(8):
                value = jnp.where(inside, 0.0, spread_row(panels[e], j))
                value = jnp.where(ones == j, 1.0, value)
                panel = panel + own[j] * value
            lines = [spread_row(panel, j) for j in range(8)]
            for g in range(8):
                at = pl.ds(8 * g, 8)
                old = grid[b, h, at, :]
                total = jnp.where(inside, 0.0, old)
                for j in range(8):
                    total = total - pick(old, start + 8 * k + j) * lines[j]
                grid[b, h, at, :] = total
            grid[b, h, here, :] = panel
        return carry

    lax.fori_loop(0, 8, block, 0)


def kernel(
    forcing_hbm, initial_hbm, blocks_hbm, faces_hbm, strength_hbm, strong_hbm, colour_hbm, near_hbm,
    out,
    forcing, initial, blocks, faces, strength, strong, colour, near, load_sem,
    rows, loose, state, cross, halo, grid, couple, known, partial, spread, send_sem, recv_sem,
):
    gx, gy = lax.axis_index("gx"), lax.axis_index("gy")
    nx, ny = lax.axis_size("gx"), lax.axis_size("gy")

    def device(dx, dy):
        return (lax.rem(gx + nx + dx, nx), lax.rem(gy + ny + dy, ny))

    def exists(dx, dy):
        return (gx + dx >= 0) & (gx + dx < nx) & (gy + dy >= 0) & (gy + dy < ny)

    sides = ((-1, 0), (1, 0), (0, -1), (0, 1))
    barrier = pltpu.get_barrier_semaphore()
    for side in sides:

        @pl.when(exists(*side))
        def _(side=side):
            pl.semaphore_signal(
                barrier, inc=1, device_id=device(*side), device_id_type=MESH
            )

    loads = [
        pltpu.make_async_copy(source, target, load_sem.at[i])
        for i, (source, target) in enumerate(
            [
                (strength_hbm, strength), (strong_hbm, strong), (colour_hbm, colour), (near_hbm, near),
                (initial_hbm, initial), (blocks_hbm, blocks), (forcing_hbm, forcing), (faces_hbm, faces),
            ]
        )
    ]
    for load in loads:
        load.start()

    left = left_lanes((N, 128))
    blank = jnp.zeros((N, 128), F32)

    def y_copy(t, b, h):
        slot = 2 * (1 - b) + h
        return pltpu.make_async_remote_copy(
            src_ref=state.at[t, b, h],
            dst_ref=halo.at[t, slot],
            send_sem=send_sem.at[t, slot],
            recv_sem=recv_sem.at[t, slot],
            device_id=device(0, 2 * b - 1),
            device_id_type=MESH,
        )

    def x_copy(t, side):
        return pltpu.make_async_remote_copy(
            src_ref=cross.at[t, side],
            dst_ref=halo.at[t, 5 - side],
            send_sem=send_sem.at[t, 5 - side],
            recv_sem=recv_sem.at[t, 5 - side],
            device_id=device(2 * side - 1, 0),
            device_id_type=MESH,
        )

    def y_start(t, b, h):
        @pl.when(exists(0, 2 * b - 1))
        def _():
            y_copy(t, b, h).start()

    def x_start(t):
        cross[t, 0] = jnp.where(left, state[t, 0, 0], swap(state[t, 1, 0]))
        cross[t, 1] = jnp.where(left, swap(state[t, 0, 1]), state[t, 1, 1])
        for side in range(2):

            @pl.when(exists(2 * side - 1, 0))
            def _(side=side):
                x_copy(t, side).start()

    nothing = jnp.zeros((STEPS, 2, N, 128), F32)
    for b in range(2):

        @pl.when(jnp.logical_not(exists(0, 2 * b - 1)))
        def _(b=b):
            halo[:, pl.ds(2 * b, 2)] = nothing

        @pl.when(jnp.logical_not(exists(2 * b - 1, 0)))
        def _(b=b):
            halo[:, 4 + b] = nothing[:, 0]

    for load in loads[:4]:
        load.wait()
    lane = lax.broadcasted_iota(jnp.int32, (8, 128), 1)
    column = lax.broadcasted_iota(jnp.int32, (8, 128), 0)
    loose[...] = jnp.zeros_like(loose)
    for a in range(4):
        for b in range(2):
            weight = jnp.where(
                near[a, b] == 48, 0.0, strength[a, b] * strong[a, b].astype(F32)
            )
            for s in range(2):
                loose[s, pl.ds(2 * a + b, 1), pl.ds(0, 6)] = weight[s : s + 1]
            loose[2, pl.ds(2 * a + b, 1), pl.ds(0, 4)] = colour[b, 0:1].astype(F32)
    painted = pick(loose[2], column // 2)
    for c in range(2):
        weight = jnp.where(painted == c, loose[0], loose[1])
        for i, face in enumerate((0, 4, 2)):
            rows[pl.ds(8 * c, 8), pl.ds(128 * i, 128)] = pick(weight, lane // N + face)
    rows[pl.ds(0, 8), pl.ds(384, 128)] = painted

    loads[4].wait()
    for b in range(2):
        for h in range(2):
            unpack_pair(initial, rows, state.at[0], b, h, 1.0)
    for load in loads[5:]:
        load.wait()
    for i, face in enumerate((0, 4, 2)):
        high, low = parts(jnp.concatenate([faces[face], faces[face + 1]], axis=1))
        for half in range(2):
            at = pl.ds(half * N, N)
            spread[at, pl.ds(128 * i, 128)] = high
            spread[at, pl.ds(384 + 128 * i, 128)] = low

    def greet():
        pl.semaphore_wait(barrier, sum(jnp.where(exists(*side), 1, 0) for side in sides))
        for b in range(2):
            for h in range(2):
                y_start(0, b, h)
        x_start(0)

    def setup(c):
        paint = c.astype(F32)
        for b in range(2):
            for h in range(2):
                unpack_pair(blocks, rows, grid, b, h, paint)
                unpack_pair(forcing, rows, known.at[c], b, h, paint)

        def visit(k):
            @pl.when((c == 0) & (k == GREET))
            def _():
                greet()

        invert(grid, visit)
        for b in range(2):
            for h in range(2):
                inverse = grid[b, h]
                stacked = jnp.concatenate(
                    [jnp.where(left, inverse, 0.0), jnp.where(left, 0.0, inverse)], axis=0
                )
                high, low = parts(stacked)
                operand = jnp.concatenate([high, low], axis=0)
                folded = jnp.dot(operand, spread[...], preferred_element_type=F32)
                mixed = folded[:128, :384] + (folded[128:, :384] + folded[:128, 384:])
                high, low = parts(known[c, b, h])
                target = jnp.concatenate([high, low], axis=1)
                folded = jnp.dot(
                    operand,
                    jnp.concatenate([target, target], axis=0),
                    preferred_element_type=F32,
                )
                mixed_known = folded[:128, :128] + (folded[128:, :128] + folded[:128, 128:])
                known[c, b, h] = jnp.where(left, mixed_known[:N], mixed_known[N:])
                for low_x in range(2):
                    weight = rows[pl.ds(8 * c + (2 * h + low_x) * 2 + b, 1), pl.ds(0, 384)]
                    scaled = mixed[N * low_x : N * low_x + N] * weight
                    if b == 0:
                        scaled = jnp.concatenate(
                            [scaled[:, :256], swap(scaled[:, 256:])], axis=1
                        )
                    high, low = parts(scaled)
                    couple[c, b, h, pl.ds(128 * low_x, N), :] = high
                    couple[c, b, h, pl.ds(128 * low_x + N, N), :] = low

    later = lax.rem(gy + 1, 2)

    def sweep(t, carry):
        c = lax.rem(t, 2)

        @pl.when(t < 2)
        def _():
            setup(c)

        for b in range(2):
            for h in range(2):
                own = state[t, b, h]
                beside = jnp.concatenate([own, own, state[t, 1 - b, h], blank], axis=0)
                partial[b, h] = known[c, b, h] - product(
                    couple[c, b, h, :, pl.ds(128, 256)], beside
                )
        for side in range(2):

            @pl.when(exists(2 * side - 1, 0))
            def _(side=side):
                x_copy(t, 1 - side).wait_recv()

        for b in range(2):
            one, two = state[t, b, 0], state[t, b, 1]
            before, after = halo[t, 4], halo[t, 5]
            if b == 0:
                after = swap(after)
            else:
                before = swap(before)
            slides = [
                jnp.where(left, before, swap(one)),
                swap(jnp.where(left, two, one)),
                jnp.where(left, swap(two), after),
            ]
            for h in range(2):
                beside = jnp.concatenate([slides[h], slides[h + 1]], axis=0)
                partial[b, h] = partial[b, h] - product(
                    couple[c, b, h, :, pl.ds(0, 128)], beside
                )
        for i in range(2):
            b = lax.rem(later + i, 2)

            @pl.when(exists(0, 2 * b - 1))
            def _(b=b):
                for h in range(2):
                    y_copy(t, 1 - b, h).wait_recv()

            for h in range(2):
                beside = jnp.concatenate([blank, halo[t, 2 * b + h]], axis=0)
                state[t + 1, b, h] = partial[b, h] - product(
                    couple[c, b, h, :, pl.ds(256, 128)], beside
                )

                @pl.when(t < STEPS - 1)
                def _(b=b, h=h):
                    y_start(t + 1, b, h)

        @pl.when(t < STEPS - 1)
        def _():
            x_start(t + 1)

        return carry

    lax.fori_loop(0, STEPS, sweep, 0)

    small = left_lanes((32, 128))
    for b in range(2):
        for h in range(2):
            values = []
            for c in range(2):
                even = state[STEPS - 1 + c, b, h, pl.ds(0, 32, stride=2), :]
                odd = state[STEPS - 1 + c, b, h, pl.ds(1, 32, stride=2), :]
                values.append(
                    (jnp.where(small, even, swap(odd)), jnp.where(small, swap(even), odd))
                )
            for low_x in range(2):
                a = 2 * h + low_x
                first = rows[pl.ds(a * 2 + b, 1), pl.ds(384, 128)]
                first = jnp.broadcast_to(first, (32, 128)) == 0.0
                zero, one = values[0][low_x], values[1][low_x]
                out[a, b, pl.ds(0, 32, stride=2), :] = jnp.where(first, zero, one)
                out[a, b, pl.ds(1, 32, stride=2), :] = jnp.where(first, one, zero)

    def drain(t, carry):
        for b in range(2):

            @pl.when(exists(0, 2 * b - 1))
            def _(b=b):
                for h in range(2):
                    y_copy(t, b, h).wait_send()

            @pl.when(exists(2 * b - 1, 0))
            def _(b=b):
                x_copy(t, b).wait_send()

        return carry

    lax.fori_loop(0, STEPS, drain, 0)


def body(forcing, initial, blocks, face_blocks, strength, strong, colour, neighbours):
    sx, sy, sz, width = forcing.shape
    chunks = width // 128

    def packed(array):
        split = array.reshape(sx, sy, sz, chunks, 128).transpose(0, 1, 3, 2, 4)
        return split.reshape(sx, sy, chunks * sz, 128)

    far = pl.BlockSpec(memory_space=pltpu.HBM)
    large = (sx, sy, chunks * sz, 128)
    result = pl.pallas_call(
        kernel,
        out_shape=jax.ShapeDtypeStruct(large, F32),
        in_specs=[far] * 8,
        out_specs=pl.BlockSpec(memory_space=pltpu.VMEM),
        scratch_shapes=[
            pltpu.VMEM(large, F32),
            pltpu.VMEM(large, F32),
            pltpu.VMEM(large, F32),
            pltpu.VMEM((6, N, N), F32),
            pltpu.VMEM((sx, sy, sz, 6), F32),
            pltpu.VMEM((sx, sy, sz, 6), jnp.int32),
            pltpu.VMEM((sy, sz, sx), jnp.int32),
            pltpu.VMEM((sx, sy, sz, 6), jnp.int32),
            pltpu.SemaphoreType.DMA((8,)),
            pltpu.VMEM((16, 512), F32),
            pltpu.VMEM((3, 8, 128), F32),
            pltpu.VMEM((STEPS + 1, 2, 2, N, 128), F32),
            pltpu.VMEM((STEPS, 2, N, 128), F32),
            pltpu.VMEM((STEPS, 6, N, 128), F32),
            pltpu.VMEM((2, 2, N, 128), F32),
            pltpu.VMEM((2, 2, 2, 4 * N, 6 * N), BF16),
            pltpu.VMEM((2, 2, 2, N, 128), F32),
            pltpu.VMEM((2, 2, N, 128), F32),
            pltpu.VMEM((2 * N, 12 * N), BF16),
            pltpu.SemaphoreType.DMA((STEPS, 6)),
            pltpu.SemaphoreType.DMA((STEPS, 6)),
        ],
        compiler_params=pltpu.CompilerParams(
            collective_id=0, has_side_effects=True, vmem_limit_bytes=65280 * 2**10
        ),
    )(
        packed(forcing),
        packed(initial),
        packed(blocks),
        face_blocks,
        strength.transpose(1, 2, 3, 0),
        strong.transpose(1, 2, 3, 0),
        colour.transpose(1, 2, 0),
        neighbours.transpose(1, 2, 3, 0),
    )
    result = result.reshape(sx, sy, chunks, sz, 128).transpose(0, 1, 3, 2, 4)
    return result.reshape(sx, sy, sz, width)


def solution(mesh):
    in_specs = (
        P("gx", "gy", None, None),
        P("gx", "gy", None, None),
        P("gx", "gy", None, None),
        P(),
        P(None, "gx", "gy", None),
        P(None, "gx", "gy", None),
        P("gx", "gy", None),
        P(None, "gx", "gy", None),
    )
    out_specs = P("gx", "gy", None, None)
    return jax.shard_map(body, mesh=mesh, in_specs=in_specs, out_specs=out_specs, check_vma=False)
```

time: 82.5 us -> 62.1 us (0.75)
  the two profiles are of different devices: /device:TPU:6 before, /device:TPU:256 now
where the time goes in v1:
time: 62.1 us; the launch traced here: 62 us
  Pallas kernels  60.3 us (97%)
  local copies, waits for them, and re-layouts  1.67 us (3%)
    pallas_call x1, Pallas kernels, body(): pl.pallas_call(kernel, out_shape=jax.ShapeDtypeStruct(large, F32), in_spe...  60.3 us
    unnamed x1, local copies, waits for them, and re-layouts  1.67 us

profile of v1, /device:TPU:256, one launch (start us, length us, event | category | flops | bytes accessed | tf_op | source)
XLA Modules:
  0.0 62.0 jit_solution(11490476295813953610)
XLA Ops:
  0.0 60.3 %shard_map.82 = f32[4,2,64,128]{3,2,1,0:T(8,128)} custom-call(f32[4,2,64,128]{3,2,1,0:T(8,128)} %bitcast.25, f32[4,2,64,128]{3,2,1,0:T(8,128)} %bitcast.26, f32[4,2,64,128]{3,2,1,0:T(8,128)} %bitcast.27, f32[6,64,64]{2,1,0:T(8,128)} %faces_hbm.1, f32[4,2,2,6]{3,2,1,0:T(2,128)} %bitcast.28, s32[4,2,2,6]{3,2,1,0:T(2,128)} %bitcast.29, s32[2,2,4]{2,1,0:T(2,128)} %bitcast.31, ...), custom_call_target="tpu_custom_call" | custom-call | tf_op jit(solution)/shard_map/pallas_call | solution.py:389
  60.3 1.7 %copy.14 = f32[4,2,2,4096]{3,2,1,0:T(2,128)} copy(f32[4,2,2,4096]{3,2,1,0:T(2,128)} %bitcast.24) | data formatting | bytes 524288

commit v2 on v1

--- a/solution.py
+++ b/solution.py
@@ -34,14 +34,14 @@
     return high, (value - high.astype(F32)).astype(BF16)
 
 
-def product(operand, value):
+def triple(value):
     high, low = parts(value)
-    total = jnp.dot(
-        operand, jnp.concatenate([high, low], axis=1), preferred_element_type=F32
-    )
-    first = total[:N, :128] + (total[N:128, :128] + total[:N, 128:])
-    second = total[128:192, :128] + (total[192:, :128] + total[128:192, 128:])
-    return jnp.where(left_lanes((N, 128)), first, second)
+    return jnp.concatenate([high, high, low], axis=0)
+
+
+def product(operand, lines):
+    total = jnp.dot(operand, lines, preferred_element_type=F32)
+    return jnp.where(left_lanes((N, 128)), total[:N], total[N:])
 
 
 def unpack_pair(source, rows, target, b, h, paint):
@@ -64,6 +64,13 @@
     within = lax.rem(lane, N)
     start = lane - within
     segment = within // 16
+    left = lane < N
+    wide = lax.broadcasted_iota(jnp.int32, (N, 128), 1)
+    slot = wide // 16
+    first = (slot == 0) | (slot == 1) | (slot == 3)
+    second = (slot == 2) | (slot == 4)
+    third = slot == 5
+    base = jnp.where(lax.rem(wide, 16) < 8, 0, N) + lax.rem(wide, 8)
 
     def block(k, carry):
         visit(k)
@@ -76,31 +83,43 @@
             for e in range(3):
                 column = jnp.where(segment == e, pick(panels[e], index), column)
             columns.append(column)
-        for k2 in range(8):
-            pivots = [spread_row(column, k2) for column in columns]
-            scale = 1.0 / pivots[k2]
-            factor = columns[k2]
+        operands = []
+        for b, h in places:
+            value = pick(grid[b, h], base + 8 * k)
+            part1 = value.astype(BF16).astype(F32)
+            part2 = (value - part1).astype(BF16).astype(F32)
+            part3 = value - part1 - part2
+            operand = jnp.where(third, part3, 0.0)
+            operand = jnp.where(first, part1, jnp.where(second, part2, operand))
+            operands.append(operand.astype(BF16))
+        for pivot in range(8):
+            lines = [spread_row(column, pivot) for column in columns]
+            scale = 1.0 / lines[pivot]
+            factor = columns[pivot]
             for j in range(8):
-                scaled = scale if j == k2 else pivots[j] * scale
-                rest = -(factor * scaled) if j == k2 else columns[j] - factor * scaled
-                columns[j] = jnp.where(row == k2, scaled, rest)
+                scaled = scale if j == pivot else lines[j] * scale
+                rest = -(factor * scaled) if j == pivot else columns[j] - factor * scaled
+                columns[j] = jnp.where(row == pivot, scaled, rest)
         inside = (within >= 8 * k) & (within < 8 * k + 8)
-        ones = within - 8 * k
+        inside_wide = (lax.rem(wide, N) >= 8 * k) & (lax.rem(wide, N) < 8 * k + 8)
         for e, (b, h) in enumerate(places):
-            own = [pick(column, start + 16 * e) for column in columns]
             panel = jnp.zeros((8, 128), F32)
             for j in range(8):
-                value = jnp.where(inside, 0.0, spread_row(panels[e], j))
-                value = jnp.where(ones == j, 1.0, value)
-                panel = panel + own[j] * value
-            lines = [spread_row(panel, j) for j in range(8)]
-            for g in range(8):
-                at = pl.ds(8 * g, 8)
-                old = grid[b, h, at, :]
-                total = jnp.where(inside, 0.0, old)
-                for j in range(8):
-                    total = total - pick(old, start + 8 * k + j) * lines[j]
-                grid[b, h, at, :] = total
+                unit = jnp.where(within == 8 * k + j, 1.0, 0.0)
+                value = jnp.where(inside, unit, spread_row(panels[e], j))
+                panel = panel + pick(columns[j], start + 16 * e) * value
+            both = jnp.concatenate(
+                [jnp.where(left, panel, 0.0), jnp.where(left, 0.0, panel)], axis=0
+            )
+            part1 = both.astype(BF16)
+            rest = both - part1.astype(F32)
+            part2, part3 = parts(rest)
+            nothing = jnp.zeros((32, 128), BF16)
+            lines = jnp.concatenate(
+                [part1, part2, part1, part3, part2, part1, nothing], axis=0
+            )
+            update = jnp.dot(operands[e], lines, preferred_element_type=F32)
+            grid[b, h] = jnp.where(inside_wide, 0.0, grid[b, h]) - update
             grid[b, h, here, :] = panel
         return carry
 
@@ -145,7 +164,7 @@
         load.start()
 
     left = left_lanes((N, 128))
-    blank = jnp.zeros((N, 128), F32)
+    blank = jnp.zeros((N, 128), BF16)
 
     def y_copy(t, b, h):
         slot = 2 * (1 - b) + h
@@ -220,11 +239,8 @@
     for load in loads[5:]:
         load.wait()
     for i, face in enumerate((0, 4, 2)):
-        high, low = parts(jnp.concatenate([faces[face], faces[face + 1]], axis=1))
-        for half in range(2):
-            at = pl.ds(half * N, N)
-            spread[at, pl.ds(128 * i, 128)] = high
-            spread[at, pl.ds(384 + 128 * i, 128)] = low
+        both = jnp.concatenate([faces[face], faces[face + 1]], axis=1)
+        spread[:, pl.ds(128 * i, 128)] = triple(jnp.concatenate([both, both], axis=0))
 
     def greet():
         pl.semaphore_wait(barrier, sum(jnp.where(exists(*side), 1, 0) for side in sides))
@@ -253,28 +269,32 @@
                     [jnp.where(left, inverse, 0.0), jnp.where(left, 0.0, inverse)], axis=0
                 )
                 high, low = parts(stacked)
-                operand = jnp.concatenate([high, low], axis=0)
-                folded = jnp.dot(operand, spread[...], preferred_element_type=F32)
-                mixed = folded[:128, :384] + (folded[128:, :384] + folded[:128, 384:])
-                high, low = parts(known[c, b, h])
-                target = jnp.concatenate([high, low], axis=1)
-                folded = jnp.dot(
-                    operand,
-                    jnp.concatenate([target, target], axis=0),
-                    preferred_element_type=F32,
-                )
-                mixed_known = folded[:128, :128] + (folded[128:, :128] + folded[:128, 128:])
-                known[c, b, h] = jnp.where(left, mixed_known[:N], mixed_known[N:])
+                operand = jnp.concatenate([high, low, high], axis=1)
+                target = known[c, b, h]
+                lines = triple(jnp.concatenate([target, target], axis=0))
+                known[c, b, h] = product(operand, lines)
+                mixed = jnp.dot(operand, spread[...], preferred_element_type=F32)
                 for low_x in range(2):
+                    at = pl.ds(N * low_x, N)
                     weight = rows[pl.ds(8 * c + (2 * h + low_x) * 2 + b, 1), pl.ds(0, 384)]
                     scaled = mixed[N * low_x : N * low_x + N] * weight
+                    beside_x, beside_z = scaled[:, :128], scaled[:, 128:256]
+                    beside_y = scaled[:, 256:]
                     if b == 0:
-                        scaled = jnp.concatenate(
-                            [scaled[:, :256], swap(scaled[:, 256:])], axis=1
-                        )
-                    high, low = parts(scaled)
-                    couple[c, b, h, pl.ds(128 * low_x, N), :] = high
-                    couple[c, b, h, pl.ds(128 * low_x + N, N), :] = low
+                        beside_y = swap(beside_y)
+                    inner = jnp.where(left, beside_z + swap(beside_z), swap(beside_y))
+                    for i, value in enumerate((inner, beside_x)):
+                        high, low = parts(value)
+                        for j, part in enumerate((high, low, high)):
+                            couple[c, b, h, at, pl.ds(384 * i + 128 * j, 128)] = part
+                    high = beside_y.astype(BF16).astype(F32)
+                    low = beside_y - high
+                    couple[c, b, h, at, pl.ds(768, 128)] = jnp.where(
+                        left, swap(high), low
+                    ).astype(BF16)
+                    couple[c, b, h, at, pl.ds(896, 128)] = jnp.where(
+                        left, swap(high), 0.0
+                    ).astype(BF16)
 
     later = lax.rem(gy + 1, 2)
 
@@ -287,10 +307,9 @@
 
         for b in range(2):
             for h in range(2):
-                own = state[t, b, h]
-                beside = jnp.concatenate([own, own, state[t, 1 - b, h], blank], axis=0)
+                beside = jnp.concatenate([state[t, b, h], state[t, 1 - b, h]], axis=0)
                 partial[b, h] = known[c, b, h] - product(
-                    couple[c, b, h, :, pl.ds(128, 256)], beside
+                    couple[c, b, h, :, pl.ds(0, 384)], triple(beside)
                 )
         for side in range(2):
 
@@ -313,20 +332,20 @@
             for h in range(2):
                 beside = jnp.concatenate([slides[h], slides[h + 1]], axis=0)
                 partial[b, h] = partial[b, h] - product(
-                    couple[c, b, h, :, pl.ds(0, 128)], beside
+                    couple[c, b, h, :, pl.ds(384, 384)], triple(beside)
                 )
         for i in range(2):
             b = lax.rem(later + i, 2)
 
-            @pl.when(exists(0, 2 * b - 1))
-            def _(b=b):
-                for h in range(2):
+            for h in range(2):
+
+                @pl.when(exists(0, 2 * b - 1))
+                def _(b=b, h=h):
                     y_copy(t, 1 - b, h).wait_recv()
 
-            for h in range(2):
-                beside = jnp.concatenate([blank, halo[t, 2 * b + h]], axis=0)
+                lines = jnp.concatenate([triple(halo[t, 2 * b + h]), blank], axis=0)
                 state[t + 1, b, h] = partial[b, h] - product(
-                    couple[c, b, h, :, pl.ds(256, 128)], beside
+                    couple[c, b, h, :, pl.ds(768, 256)], lines
                 )
 
                 @pl.when(t < STEPS - 1)
@@ -407,10 +426,10 @@
             pltpu.VMEM((STEPS, 2, N, 128), F32),
             pltpu.VMEM((STEPS, 6, N, 128), F32),
             pltpu.VMEM((2, 2, N, 128), F32),
-            pltpu.VMEM((2, 2, 2, 4 * N, 6 * N), BF16),
+            pltpu.VMEM((2, 2, 2, 2 * N, 1024), BF16),
             pltpu.VMEM((2, 2, 2, N, 128), F32),
             pltpu.VMEM((2, 2, N, 128), F32),
-            pltpu.VMEM((2 * N, 12 * N), BF16),
+            pltpu.VMEM((6 * N, 6 * N), BF16),
             pltpu.SemaphoreType.DMA((STEPS, 6)),
             pltpu.SemaphoreType.DMA((STEPS, 6)),
         ],

time: 62.1 us -> 51.1 us (0.82)
  the two profiles are of different devices: /device:TPU:256 before, /device:TPU:120 now
where the time goes in v2:
time: 51.1 us; the launch traced here: 50.9 us
  Pallas kernels  49.2 us (96%)
  local copies, waits for them, and re-layouts  1.67 us (3%)
    pallas_call x1, Pallas kernels, body(): pl.pallas_call(kernel, out_shape=jax.ShapeDtypeStruct(large, F32), in_spe...  49.2 us
    unnamed x1, local copies, waits for them, and re-layouts  1.67 us

profile of v2, /device:TPU:120, one launch (start us, length us, event | category | flops | bytes accessed | tf_op | source)
XLA Modules:
  0.0 50.9 jit_solution(5317485239648585540)
XLA Ops:
  0.0 49.2 %shard_map.82 = f32[4,2,64,128]{3,2,1,0:T(8,128)} custom-call(f32[4,2,64,128]{3,2,1,0:T(8,128)} %bitcast.25, f32[4,2,64,128]{3,2,1,0:T(8,128)} %bitcast.26, f32[4,2,64,128]{3,2,1,0:T(8,128)} %bitcast.27, f32[6,64,64]{2,1,0:T(8,128)} %faces_hbm.1, f32[4,2,2,6]{3,2,1,0:T(2,128)} %bitcast.28, s32[4,2,2,6]{3,2,1,0:T(2,128)} %bitcast.29, s32[2,2,4]{2,1,0:T(2,128)} %bitcast.31, ...), custom_call_target="tpu_custom_call" | custom-call | tf_op jit(solution)/shard_map/pallas_call | solution.py:408
  49.3 1.7 %copy.14 = f32[4,2,2,4096]{3,2,1,0:T(2,128)} copy(f32[4,2,2,4096]{3,2,1,0:T(2,128)} %bitcast.24) | data formatting | bytes 524288

commit v3 on v2

--- a/solution.py
+++ b/solution.py
@@ -434,17 +434,22 @@
             pltpu.SemaphoreType.DMA((STEPS, 6)),
         ],
         compiler_params=pltpu.CompilerParams(
-            collective_id=0, has_side_effects=True, vmem_limit_bytes=65280 * 2**10
+            collective_id=0, has_side_effects=True, vmem_limit_bytes=40000 * 2**10
         ),
     )(
-        packed(forcing),
-        packed(initial),
-        packed(blocks),
-        face_blocks,
-        strength.transpose(1, 2, 3, 0),
-        strong.transpose(1, 2, 3, 0),
-        colour.transpose(1, 2, 0),
-        neighbours.transpose(1, 2, 3, 0),
+        *(
+            pltpu.with_memory_space_constraint(array, pltpu.HBM)
+            for array in (
+                packed(forcing),
+                packed(initial),
+                packed(blocks),
+                face_blocks,
+                strength.transpose(1, 2, 3, 0),
+                strong.transpose(1, 2, 3, 0),
+                colour.transpose(1, 2, 0),
+                neighbours.transpose(1, 2, 3, 0),
+            )
+        )
     )
     result = result.reshape(sx, sy, chunks, sz, 128).transpose(0, 1, 3, 2, 4)
     return result.reshape(sx, sy, sz, width)

time: 51.1 us -> 49.4 us (0.967)
  local copies, waits for them, and re-layouts: 1.67 us -> 0.71 us
  Pallas kernels: 49.2 us -> 48.6 us
    unnamed x1, local copies, waits for them, and re-layouts: 1.67 us -> 0.71 us
    pallas_call x1, Pallas kernels: 49.2 us -> 48.6 us  [body(): pl.pallas_call(kernel, out_shape=jax.ShapeDtypeStruct(large, F32), in_spe...]
where the time goes in v3:
time: 49.4 us; the launch traced here: 49.3 us
  Pallas kernels  48.6 us (98%)
  local copies, waits for them, and re-layouts  0.71 us (1%)
    pallas_call x1, Pallas kernels, body(): pl.pallas_call(kernel, out_shape=jax.ShapeDtypeStruct(large, F32), in_spe...  48.6 us

profile of v3, /device:TPU:120, one launch (start us, length us, event | category | flops | bytes accessed | tf_op | source)
XLA Modules:
  0.0 49.3 jit_solution(11437681952219033115)
XLA Ops:
  0.0 48.6 %shard_map.82 = f32[4,2,64,128]{3,2,1,0:T(8,128)S(1)} custom-call(f32[4,2,64,128]{3,2,1,0:T(8,128)} %bitcast.25, f32[4,2,64,128]{3,2,1,0:T(8,128)} %bitcast.26, f32[4,2,64,128]{3,2,1,0:T(8,128)} %bitcast.27, f32[6,64,64]{2,1,0:T(8,128)} %faces_hbm.1, f32[4,2,2,6]{3,2,1,0:T(2,128)} %bitcast.28, s32[4,2,2,6]{3,2,1,0:T(2,128)} %bitcast.29, ...), custom_call_target="tpu_custom_call" | custom-call | tf_op jit(solution)/shard_map/pallas_call | solution.py:408
  48.6 0.7 %copy.14 = f32[4,2,2,4096]{3,2,1,0:T(2,128)} copy(f32[4,2,2,4096]{3,2,1,0:T(2,128)S(1)} %bitcast.24) | data formatting | bytes 524288

commit v4 on v3

--- a/solution.py
+++ b/solution.py
@@ -298,6 +298,18 @@
 
     later = lax.rem(gy + 1, 2)
 
+    def drain(t):
+        for b in range(2):
+
+            @pl.when(exists(0, 2 * b - 1))
+            def _(b=b):
+                for h in range(2):
+                    y_copy(t, b, h).wait_send()
+
+            @pl.when(exists(2 * b - 1, 0))
+            def _(b=b):
+                x_copy(t, b).wait_send()
+
     def sweep(t, carry):
         c = lax.rem(t, 2)
 
@@ -356,6 +368,7 @@
         def _():
             x_start(t + 1)
 
+        drain(t)
         return carry
 
     lax.fori_loop(0, STEPS, sweep, 0)
@@ -377,22 +390,6 @@
                 zero, one = values[0][low_x], values[1][low_x]
                 out[a, b, pl.ds(0, 32, stride=2), :] = jnp.where(first, zero, one)
                 out[a, b, pl.ds(1, 32, stride=2), :] = jnp.where(first, one, zero)
-
-    def drain(t, carry):
-        for b in range(2):
-
-            @pl.when(exists(0, 2 * b - 1))
-            def _(b=b):
-                for h in range(2):
-                    y_copy(t, b, h).wait_send()
-
-            @pl.when(exists(2 * b - 1, 0))
-            def _(b=b):
-                x_copy(t, b).wait_send()
-
-        return carry
-
-    lax.fori_loop(0, STEPS, drain, 0)
 
 
 def body(forcing, initial, blocks, face_blocks, strength, strong, colour, neighbours):

time: 49.4 us -> 49.3 us (level)
  no operation moved by 1% of the time
where the time goes in v4:
time: 49.3 us; the launch traced here: 49.1 us
  Pallas kernels  48.4 us (98%)
  local copies, waits for them, and re-layouts  0.71 us (1%)
    pallas_call x1, Pallas kernels, body(): pl.pallas_call(kernel, out_shape=jax.ShapeDtypeStruct(large, F32), in_spe...  48.4 us

profile of v4, /device:TPU:120, one launch (start us, length us, event | category | flops | bytes accessed | tf_op | source)
XLA Modules:
  0.0 49.1 jit_solution(9802239641193298484)
XLA Ops:
  0.0 48.4 %shard_map.82 = f32[4,2,64,128]{3,2,1,0:T(8,128)S(1)} custom-call(f32[4,2,64,128]{3,2,1,0:T(8,128)} %bitcast.25, f32[4,2,64,128]{3,2,1,0:T(8,128)} %bitcast.26, f32[4,2,64,128]{3,2,1,0:T(8,128)} %bitcast.27, f32[6,64,64]{2,1,0:T(8,128)} %faces_hbm.1, f32[4,2,2,6]{3,2,1,0:T(2,128)} %bitcast.28, s32[4,2,2,6]{3,2,1,0:T(2,128)} %bitcast.29, ...), custom_call_target="tpu_custom_call" | custom-call | tf_op jit(solution)/shard_map/pallas_call | solution.py:405
  48.4 0.7 %copy.14 = f32[4,2,2,4096]{3,2,1,0:T(2,128)} copy(f32[4,2,2,4096]{3,2,1,0:T(2,128)S(1)} %bitcast.24) | data formatting | bytes 524288
